TPU v7x, 128 devices: a whole 4x4x4 slice. The times are simulated.
128 devices in a mesh: section: 32 (over z, y, core), tensor: 4 (over x).
Axes of the slice: x: 4, y: 4, z: 4, core: 2. Of those that a mesh axis runs over, the one named last changes fastest.
Arguments:
- flight_state: bfloat16 [32, 512, 3584], P('section', 'tensor'), may hold values from -6 to 6
- flight_tokens: int32 [32, 3], P('section'), may hold values from 1 to 256, as said below
- flight_lists: int32 [32, 3], P('section'), may hold values from 0 to 1023, as said below
- incoming: bfloat16 [2, 512, 3584], P(None, 'tensor'), may hold values from -6 to 6
- incoming_tokens: int32 [2, 3], replicated, may hold values from 1 to 256, as said below
- norm_gain: float32 [32, 3584], P('section'), may hold values from 0.25 to 1.75
- query_weight: bfloat16 [32, 3584, 3584], P('section', None, 'tensor'), may hold values from -0.09375 to 0.09375
- query_bias: float32 [32, 3584], P('section', 'tensor'), may hold values from -10 to 10
- key_weight: bfloat16 [32, 3584, 512], P('section', None, 'tensor'), may hold values from -0.09375 to 0.09375
- key_bias: float32 [32, 512], P('section', 'tensor'), may hold values from -10 to 10
- value_weight: bfloat16 [32, 3584, 512], P('section', None, 'tensor'), may hold values from -0.09375 to 0.09375
- value_bias: float32 [32, 512], P('section', 'tensor'), may hold values from -3 to 3
- output_weight: bfloat16 [32, 3584, 3584], P('section', 'tensor'), may hold values from -0.09375 to 0.09375
- list_rows: int32 [1024], replicated, may hold values from 0 to 1023, each once
Outputs:
- next_state: bfloat16 [32, 512, 3584], P('section', 'tensor')
- list_sums: float32 [1024, 3584], P(('section', 'tensor'))
Inputs may be any that keep to these rules, and one draw needn't show every extreme that they name: `flight_tokens`: in each micro-batch the blocks ceil(tokens / 128) of its 3 programs sum to 4; in every draw some program has the most and some program has 1 token. `incoming_tokens`: in each micro-batch the blocks ceil(tokens / 128) of its 3 programs sum to 4; in every draw some program has the most and some program has 1 token. `flight_lists`: every micro-batch after the first gives one of its programs the list of some program of the micro-batch before it.
All inputs are finite; a program needn't handle non-finite values.
Results may differ from a plain program's by a relative error of at most 0.034.
Values may be sent and summed in bfloat16 or wider, within the bound.
A program may use at most 128 MiB of HBM per device.

v0:
```python
import math
import jax
import jax.numpy as jnp
from jax import lax
from jax.sharding import PartitionSpec as P

HEAD = 128
LAYERS = 28
BLOCK = 128
EPS = 1e-06
THETA = 1000000.0


def from_behind(block, axis, distance):
    devices = range(lax.axis_size(axis))
    route = [((i - distance) % len(devices), i) for i in devices]
    return lax.ppermute(block, axis, route)


def broadcast(value, axis, root):
    mine = lax.axis_index(axis) == root
    return lax.psum(jnp.where(mine, value, jnp.zeros_like(value)), axis)


def as_sent(value):
    return jax.tree.map(lambda a: a.astype(jnp.bfloat16) if a.dtype == jnp.float32 else a, value)


def row_layout(tokens, first, count):
    blocks = (tokens + BLOCK - 1) // BLOCK
    ends = (jnp.cumsum(blocks) * BLOCK).astype(jnp.int32)
    starts = ends - blocks * BLOCK
    slots = first + jnp.arange(count, dtype=jnp.int32)
    program = jnp.sum((slots[:, None] >= ends[None, :]).astype(jnp.int32), axis=1)
    chosen = program[:, None] == jnp.arange(tokens.shape[0], dtype=jnp.int32)[None, :]
    begin = jnp.sum(jnp.where(chosen, starts[None, :], 0), axis=1)
    length = jnp.sum(jnp.where(chosen, tokens[None, :], 0), axis=1)
    position = slots - begin
    return (program, position, position < length)


def rotate(values, position):
    half = values.shape[-1] // 2
    freq = THETA ** (-jnp.arange(half, dtype=jnp.float32) * 2.0 / values.shape[-1])
    angle = position.astype(jnp.float32)[:, None] * freq[None, :]
    cosine = jnp.cos(angle)[:, None, :]
    sine = jnp.sin(angle)[:, None, :]
    first_half = values[..., :half]
    second_half = values[..., half:]
    return jnp.concatenate(
        [first_half * cosine - second_half * sine, second_half * cosine + first_half * sine],
        axis=-1,
    )


def attend(queries, key_rows, value_rows, program, valid):
    total = queries.shape[0]
    width = min(512, total)
    scale = 1.0 / math.sqrt(queries.shape[-1])

    def one_block(index):
        scores = (
            jnp.einsum("qcgd,kcd->cgqk", queries, key_rows, preferred_element_type=jnp.float32)
            * scale
        )
        allowed = (program[:, None] == program[None, :]) & valid[None, :]
        scores = jnp.where(allowed[None, None], scores, -1e30)
        top = jnp.max(scores, axis=-1, keepdims=True)
        expo = jnp.exp(scores - top)
        probs = (expo / jnp.sum(expo, axis=-1, keepdims=True)).astype(jnp.bfloat16)
        mixed = jnp.einsum("cgqk,kcd->qcgd", probs, value_rows, preferred_element_type=jnp.float32)
        return mixed.astype(jnp.bfloat16)

    blocks = lax.map(one_block, jnp.arange(total // width, dtype=jnp.int32))
    return blocks.reshape(total, -1)


def normalize(state, gain):
    values = state.astype(jnp.float32)
    return (
        values * lax.rsqrt(jnp.mean(values * values, axis=-1, keepdims=True) + EPS) * gain
    ).astype(jnp.bfloat16)


def local(
    flight_state,
    flight_tokens,
    flight_lists,
    incoming,
    incoming_tokens,
    norm_gain,
    query_weight,
    query_bias,
    key_weight,
    key_bias,
    value_weight,
    value_bias,
    output_weight,
    list_rows,
):
    tensor_count = lax.axis_size("tensor")
    section_count = lax.axis_size("section")
    tensor_rank = lax.axis_index("tensor")
    section_rank = lax.axis_index("section")
    is_last = section_rank == section_count - 1
    active = section_rank < min(section_count, LAYERS)
    own_rows = flight_state.shape[1]
    all_rows = own_rows * tensor_count
    row_first = tensor_rank * own_rows
    query_cols = query_weight.shape[2]
    key_cols = key_weight.shape[2]
    kv_local = key_cols // HEAD
    groups = query_cols // key_cols
    gain = norm_gain[0]
    prog_count = flight_tokens.shape[1]

    def assemble(rows):
        return lax.all_gather(rows, "tensor", axis=0, tiled=True)

    tokens = flight_tokens[0]
    lists = flight_lists[0]
    part_list = []
    token_list = []
    lists_list = []
    whole = assemble(flight_state[0])
    for tick in range(incoming.shape[0]):
        piece = normalize(whole, gain)
        combined = jnp.concatenate(
            [
                jnp.dot(piece, query_weight[0], preferred_element_type=jnp.float32),
                jnp.dot(piece, key_weight[0], preferred_element_type=jnp.float32),
                jnp.dot(piece, value_weight[0], preferred_element_type=jnp.float32),
            ],
            axis=1,
        )
        heads_program, heads_position, heads_valid = row_layout(tokens, 0, all_rows)
        query_f = combined[:, :query_cols] + query_bias[0]
        key_f = combined[:, query_cols : query_cols + key_cols] + key_bias[0]
        value_f = combined[:, query_cols + key_cols :] + value_bias[0]
        queries = rotate(query_f.reshape(all_rows, kv_local * groups, HEAD), heads_position).astype(
            jnp.bfloat16
        )
        queries = queries.reshape(all_rows, kv_local, groups, HEAD)
        key_rows = rotate(key_f.reshape(all_rows, kv_local, HEAD), heads_position).astype(
            jnp.bfloat16
        )
        value_rows = value_f.astype(jnp.bfloat16).reshape(all_rows, kv_local, HEAD)
        mixed = attend(queries, key_rows, value_rows, heads_program, heads_valid)
        rows_now = lax.dynamic_slice_in_dim(whole, row_first, own_rows, 0)
        summed = lax.psum_scatter(
            jnp.dot(mixed, output_weight[0], preferred_element_type=jnp.float32).astype(
                jnp.bfloat16
            ),
            "tensor",
            scatter_dimension=0,
            tiled=True,
        ).astype(jnp.float32)
        mapped = (rows_now.astype(jnp.float32) + summed).astype(jnp.bfloat16)
        rows_out = jnp.where(active, mapped, rows_now)
        program, position, valid = row_layout(tokens, row_first, own_rows)
        member = (
            (program[None, :] == jnp.arange(prog_count, dtype=jnp.int32)[:, None]) & valid[None, :]
        ).astype(jnp.bfloat16)
        part_list.append(jnp.dot(member, rows_out, preferred_element_type=jnp.float32))
        token_list.append(tokens)
        lists_list.append(lists)
        outgoing = jnp.where(is_last, incoming[tick], rows_out)
        sent_tokens = jnp.where(is_last, incoming_tokens[tick], tokens)
        sent_lists = jnp.where(is_last, jnp.zeros_like(lists), lists)
        whole, tokens, lists = from_behind(
            (assemble(outgoing), sent_tokens, sent_lists), "section", 1
        )
    state_rows = lax.dynamic_slice_in_dim(whole, row_first, own_rows, 0)
    parts = jnp.stack(part_list)
    counts = jnp.stack(token_list)
    exit_lists = jnp.stack(lists_list)
    total = lax.psum(parts.astype(jnp.bfloat16), "tensor").astype(jnp.float32)
    means = total / counts[..., None].astype(jnp.float32)
    embedded = means * lax.rsqrt(jnp.mean(means * means, axis=-1, keepdims=True) + EPS)
    embedded, exit_lists = (
        broadcast(embedded.astype(jnp.bfloat16), "section", section_count - 1).astype(
            embedded.dtype
        ),
        broadcast(as_sent(exit_lists), "section", section_count - 1).astype(exit_lists.dtype),
    )
    flat = embedded.reshape(-1, embedded.shape[-1])
    flat_lists = exit_lists.reshape(-1)
    list_total = list_rows.shape[0]
    target = jnp.sum(
        jnp.where(
            flat_lists[:, None] == jnp.arange(list_total, dtype=jnp.int32)[None, :],
            list_rows[None, :],
            0,
        ),
        axis=1,
    )
    local_count = list_total // (section_count * tensor_count)
    owned = lax.axis_index(("section", "tensor")) * local_count + jnp.arange(
        local_count, dtype=jnp.int32
    )
    select = (owned[:, None] == target[None, :]).astype(jnp.float32)
    list_sums = jnp.dot(select, flat, precision=lax.Precision.HIGHEST)
    return (state_rows[None], list_sums)


def solution(mesh):
    in_specs = (
        P("section", "tensor", None),
        P("section", None),
        P("section", None),
        P(None, "tensor", None),
        P(),
        P("section", None),
        P("section", None, "tensor"),
        P("section", "tensor"),
        P("section", None, "tensor"),
        P("section", "tensor"),
        P("section", None, "tensor"),
        P("section", "tensor"),
        P("section", "tensor", None),
        P(),
    )
    out_specs = (P("section", "tensor", None), P(("section", "tensor"), None))
    return jax.shard_map(local, mesh=mesh, in_specs=in_specs, out_specs=out_specs, check_vma=False)
```

profile of v0, /device:TPU:0, one launch (start us, length us, event | category | flops | bytes accessed | tf_op | source)
XLA Modules:
  0.0 579.1 jit_solution(16477160890725204429)
XLA Ops:
  7.2 0.7 all-gather.9.cloned.1.call-update
  8.0 0.7 broadcast_select_fusion.1
  8.7 0.7 reduce.5
  9.4 0.8 reduce.4
  10.2 0.7 and_select_fusion.2
  10.8 0.2 reduce-window.12
  11.1 0.7 fusion.116
  11.8 0.7 select_reduce_fusion.3
  12.6 0.2 compare_and_fusion.1
  12.8 3.1 collective-permute-done.1
  15.9 0.2 reduce-window.13
  16.3 0.5 copy-done.25
  16.8 2.7 multiply_cosine_fusion
  19.5 36.6 %all-gather.9.cloned.1.call-done = bf16[1,512,3584]{2,1,0:T(8,128)(2,1)} async-done(((bf16[1,128,3584]{2,1,0:T(8,128)(2,1)}), bf16[1,512,3584]{2,1,0:T(8,128)(2,1)}) %all-gather.9.cloned.1.call-update) | async-done | bytes 3670032 | tf_op jit(solution)/shard_map/all_gather | solution.py:118
  56.1 3.0 fusion.3
  59.1 0.1 copy-done.3
  59.2 1.5 fusion.47
  60.7 1.2 fusion.93
  61.9 0.1 copy-done.34
  62.0 5.3 fusion.32
  67.3 2.0 copy.34
  69.3 1.5 fusion.132
  70.8 1.7 copy.57
  72.5 3.0 copy.56
  75.5 2.1 subtract_convert_fusion.1
  77.6 2.1 fusion.22
  79.7 1.6 fusion.6
  81.3 1.4 copy-done.2
  82.6 7.6 %fusion.38 = bf16[128,7,512]{2,0,1:T(8,128)(2,1)S(1)} fusion(f32[7,512]{1,0:T(8,128)S(1)} %fusion.6, f32[7,512]{1,0:T(8,128)S(1)} %get-tuple-element.72, f32[512,512,7]{1,0,2:T(8,128)} %copy-done.2, pred[512,512]{0,1:T(8,128)(4,1)S(1)} %compare_and_fusion.1, bf16[1,3584,128]{2,1,0:T(8,128)(2,1)S(1)} %copy-done, f32[128]{0:T(128)S(1)} %bitcast.180, ...), kind=kOutput, calls=%fused_computation.48 | convolution fusion | flops 956628992 | bytes 13152768 | tf_op jit(solution)/shard_map/while/body/eval_jaxpr/cgqk,kcd->qcgd/dot_general | solution.py:71
  90.2 8.3 %fusion.16 = bf16[512,3584]{1,0:T(8,128)(2,1)} fusion(bf16[512,896]{0,1:T(8,128)(2,1)S(1)} %bitcast.183, bf16[1,896,3584]{2,1,0:T(8,128)(2,1)} %param.26), kind=kOutput, calls=%fused_computation.26 | convolution fusion | flops 3290169344 | bytes 11010048 | tf_op jit(solution)/shard_map/dot_general | solution.py:151
  98.6 42.9 %reduce-scatter.3.cloned.1.call-done = bf16[128,3584]{1,0:T(8,128)(2,1)} async-done(((bf16[512,3584]{1,0:T(8,128)(2,1)}), bf16[128,3584]{1,0:T(8,128)(2,1)}) %reduce-scatter.3.cloned.1.call-update) | async-done | bytes 917520 | tf_op jit(solution)/shard_map/reduce_scatter | solution.py:150
  141.5 2.8 bitcast_select_fusion.2
  144.3 43.7 %all-gather.5.cloned.1.call-done = bf16[512,3584]{1,0:T(8,128)(2,1)} async-done(((bf16[128,3584]{1,0:T(8,128)(2,1)}), bf16[512,3584]{1,0:T(8,128)(2,1)}) %all-gather.5.cloned.1.call-update) | async-done | bytes 3670032 | tf_op jit(solution)/shard_map/all_gather | solution.py:118
  188.1 0.2 collective-permute-start
  188.3 0.2 compare_and_fusion
  188.5 45.6 %collective-permute-done = bf16[512,3584]{1,0:T(8,128)(2,1)S(1)} collective-permute-done((bf16[512,3584]{1,0:T(8,128)(2,1)}, bf16[512,3584]{1,0:T(8,128)(2,1)S(1)}, u32[]{:S(2)}, u32[]{:S(2)}) %collective-permute-start) | collective-permute-done | bytes 3670048 | tf_op jit(solution)/shard_map/ppermute | solution.py:17
  234.1 0.8 fusion
  234.9 2.2 fusion.46
  237.2 1.2 fusion.95
  238.4 8.1 %fusion.35 = f32[512,896]{1,0:T(8,128)} fusion(bf16[1,3584,896]{2,1,0:T(8,128)(2,1)} %param.20, f32[896]{0:T(1024)S(1)} %copy-done.22, bf16[512,3584]{1,0:T(8,128)(2,1)S(1)} %collective-permute-done, f32[512]{0:T(512)S(1)} %add_rsqrt_fusion, f32[3584]{0:T(1024)S(1)} %copy-done.13), kind=kOutput, calls=%fused_computation.47 | convolution fusion | flops 3296133120 | bytes 11947520 | tf_op jit(solution)/shard_map/dot_general | solution.py:130
  246.5 1.8 copy.40
  248.3 1.5 fusion.131
  249.8 1.7 copy.59
  251.5 3.0 copy.58
  254.5 2.0 subtract_convert_fusion
  256.5 2.1 fusion.23
  258.6 3.0 copy-done.1
  261.6 1.6 fusion.7
  263.1 7.6 %fusion.41 = bf16[128,7,512]{2,0,1:T(8,128)(2,1)S(1)} fusion(f32[7,512]{1,0:T(8,128)S(1)} %fusion.7, f32[7,512]{1,0:T(8,128)S(1)} %get-tuple-element.74, f32[512,512,7]{1,0,2:T(8,128)} %copy-done.1, pred[512,512]{0,1:T(8,128)(4,1)S(1)} %compare_and_fusion, bf16[1,3584,128]{2,1,0:T(8,128)(2,1)S(1)} %copy-done, f32[128]{0:T(128)S(1)} %bitcast.181, ...), kind=kOutput, calls=%fused_computation.49 | convolution fusion | flops 956628992 | bytes 13152768 | tf_op jit(solution)/shard_map/while/body/eval_jaxpr/cgqk,kcd->qcgd/dot_general | solution.py:71
  270.7 8.3 %fusion.19 = bf16[512,3584]{1,0:T(8,128)(2,1)} fusion(bf16[512,896]{0,1:T(8,128)(2,1)S(1)} %bitcast.182, bf16[1,896,3584]{2,1,0:T(8,128)(2,1)} %param.26), kind=kOutput, calls=%fused_computation.27 | convolution fusion | flops 3290169344 | bytes 11010048 | tf_op jit(solution)/shard_map/dot_general | solution.py:151
  279.1 39.6 %reduce-scatter.5.cloned.1.call-done = bf16[128,3584]{1,0:T(8,128)(2,1)} async-done(((bf16[512,3584]{1,0:T(8,128)(2,1)}), bf16[128,3584]{1,0:T(8,128)(2,1)}) %reduce-scatter.5.cloned.1.call-update) | async-done | bytes 917520 | tf_op jit(solution)/shard_map/reduce_scatter | solution.py:150
  318.7 2.8 bitcast_select_fusion.3
  321.5 43.8 %all-gather.7.cloned.1.call-done = bf16[512,3584]{1,0:T(8,128)(2,1)} async-done(((bf16[128,3584]{1,0:T(8,128)(2,1)}), bf16[512,3584]{1,0:T(8,128)(2,1)}) %all-gather.7.cloned.1.call-update) | async-done | bytes 3670032 | tf_op jit(solution)/shard_map/all_gather | solution.py:118
  365.3 1.6 collective-permute-start.3
  366.9 44.3 %collective-permute-done.3 = s32[3]{0:T(128)S(1)} collective-permute-done((s32[3]{0:T(128)S(1)}, s32[3]{0:T(128)S(1)}, u32[]{:S(2)}, u32[]{:S(2)}) %collective-permute-start.3) | collective-permute-done | bytes 44 | tf_op jit(solution)/shard_map/ppermute | solution.py:17
  411.3 13.5 %psum.21 = s32[6]{0:T(128)S(1)} all-reduce(s32[6]{0:T(128)S(1)} %eq.173), channel_id=1, replica_groups=mesh['section'=32,'tensor'=4] {'section'}, use_global_device_ids=true, to_apply=%region_16.17 | all-reduce | flops 6 | bytes 48 | tf_op jit(solution)/shard_map/psum | solution.py:22
  424.9 0.2 select_reduce_fusion
  425.3 1.9 fusion.24
  427.2 1.8 fusion.25
  429.1 15.9 %psum.22 = bf16[2,3,3584]{2,1,0:T(4,128)(2,1)S(1)} all-reduce(bf16[2,3,3584]{2,1,0:T(4,128)(2,1)S(1)} %pad_maximum_fusion), channel_id=1, replica_groups=mesh['section'=32,'tensor'=4] {'tensor'}, use_global_device_ids=true, to_apply=%region_24.25 | all-reduce | flops 21504 | bytes 86016 | tf_op jit(solution)/shard_map/psum | solution.py:177
  445.0 0.2 multiply_reduce_fusion
  445.3 123.9 %psum.23 = bf16[6,3584]{1,0:T(8,128)(2,1)S(1)} all-reduce(bf16[6,3584]{1,0:T(8,128)(2,1)S(1)} %reshape.609), channel_id=1, replica_groups=mesh['section'=32,'tensor'=4] {'section'}, use_global_device_ids=true, to_apply=%region_26.27 | all-reduce | flops 21504 | bytes 86016 | tf_op jit(solution)/shard_map/psum | solution.py:22
  569.2 0.8 fusion.97
  570.0 2.2 dynamic-slice_bitcast_fusion
  (115 shorter events, 1.4 us)
Async XLA Ops:
  7.2 75.5 %copy-start = (bf16[1,3584,128]{2,1,0:T(8,128)(2,1)S(1)}, bf16[1,3584,128]{2,1,0:T(8,128)(2,1)}, u32[]{:S(2)}) copy-start(bf16[1,3584,128]{2,1,0:T(8,128)(2,1)} %param.24) | copy-start | bytes 2752516
  7.2 51.9 %copy-start.35 = (bf16[1,3584,128]{2,1,0:T(8,128)(2,1)S(1)}, bf16[1,3584,128]{2,1,0:T(8,128)(2,1)}, u32[]{:S(2)}) copy-start(bf16[1,3584,128]{2,1,0:T(8,128)(2,1)} %param.22) | copy-start | bytes 2752516
  7.2 51.9 %copy-start.37 = (f32[1,128]{1,0:T(1,128)S(1)}, f32[1,128]{1,0:T(1,128)}, u32[]{:S(2)}) copy-start(f32[1,128]{1,0:T(1,128)} %param.23) | copy-start | bytes 1540
  7.2 48.9 %all-gather.9.cloned.1.call-start = ((), (), s32[]{:S(2)}) async-start(), calls=%async_computation.6 | async-start | bytes 4587520 | tf_op jit(solution)/shard_map/all_gather | solution.py:118
  7.9 133.5 %reduce-scatter.3.cloned.1.call-start = ((), (), s32[]{:S(2)}) async-start(), calls=%async_computation.2 | async-start | bytes 4587520 | tf_op jit(solution)/shard_map/reduce_scatter | solution.py:150
  8.7 7.2 %collective-permute-start.1 = (s32[3]{0:T(128)S(1)}, s32[3]{0:T(128)S(1)}, u32[]{:S(2)}, u32[]{:S(2)}) collective-permute-start(s32[3]{0:T(128)S(1)} %broadcast_select_fusion.1), channel_id=1, source_target_pairs={{124,0},{0,4},{4,8},{8,12},{12,16},{16,20},{20,24},{24,28},{28,32}... | collective-permute-start | bytes 44 | tf_op jit(solution)/shard_map/ppermute | solution.py:17
  9.4 52.5 %copy-start.21 = (f32[896]{0:T(1024)}, f32[896]{0:T(1024)S(1)}, u32[]{:S(2)}) copy-start(f32[896]{0:T(1024)S(1)} %reduce.5) | copy-start | bytes 10756
  10.1 51.8 %copy-start.11 = (f32[3584]{0:T(1024)}, f32[3584]{0:T(1024)S(1)}, u32[]{:S(2)}) copy-start(f32[3584]{0:T(1024)S(1)} %reduce.4) | copy-start | bytes 43012
  11.0 49.7 %copy-start.16 = (f32[64]{0:T(128)}, f32[64]{0:T(128)S(1)}, u32[]{:S(2)}) copy-start(f32[64]{0:T(128)S(1)} %multiply_power_fusion) | copy-start | bytes 772
  11.0 0.8 copy-start.27
  11.8 0.8 copy-start.23
  15.9 3.6 copy-start.18
  16.1 0.7 copy-start.29
  16.2 0.6 copy-start.25
  56.1 3.1 copy-start.3
  59.1 2.8 copy-start.31
  59.2 2.8 copy-start.34
  75.5 2.1 copy-start.9
  75.5 2.1 copy-start.10
  79.7 3.0 copy-start.2
  79.7 3.0 copy-start.12
  79.7 3.0 copy-start.32
  79.7 3.0 copy-start.38
  98.5 43.0 %copy-start.5 = (bf16[2,128,3584]{2,1,0:T(8,128)(2,1)S(1)}, bf16[2,128,3584]{2,1,0:T(8,128)(2,1)}, u32[]{:S(2)}) copy-start(bf16[2,128,3584]{2,1,0:T(8,128)(2,1)} %param.17) | copy-start | bytes 5505028
  98.5 89.5 %all-gather.5.cloned.1.call-start = ((), (), s32[]{:S(2)}) async-start(), calls=%async_computation.3 | async-start | bytes 4587520 | tf_op jit(solution)/shard_map/all_gather | solution.py:118
  144.3 90.6 %copy-start.36 = (bf16[1,3584,128]{2,1,0:T(8,128)(2,1)S(1)}, bf16[1,3584,128]{2,1,0:T(8,128)(2,1)}, u32[]{:S(2)}) copy-start(bf16[1,3584,128]{2,1,0:T(8,128)(2,1)} %param.22) | copy-start | bytes 2752516
  144.3 174.4 %reduce-scatter.5.cloned.1.call-start = ((), (), s32[]{:S(2)}) async-start(), calls=%async_computation.4 | async-start | bytes 4587520 | tf_op jit(solution)/shard_map/reduce_scatter | solution.py:150
  188.1 46.0 %collective-permute-start = (bf16[512,3584]{1,0:T(8,128)(2,1)}, bf16[512,3584]{1,0:T(8,128)(2,1)S(1)}, u32[]{:S(2)}, u32[]{:S(2)}) collective-permute-start(bf16[512,3584]{1,0:T(8,128)(2,1)} %all-gather.5.cloned.1.call-done), channel_id=1, source_target_pairs={{124,0},{0,4},{4,8},{8,12},{12,16},{16,20},{20,24},{24,28},{28,32}... | collective-permute-start | bytes 11010056 | tf_op jit(solution)/shard_map/ppermute | solution.py:17
  234.1 4.3 copy-start.4
  234.9 2.3 copy-start.17
  234.9 3.5 copy-start.13
  234.9 3.5 copy-start.22
  254.5 2.0 copy-start.7
  254.5 2.0 copy-start.8
  258.6 3.0 copy-start.1
  261.6 1.6 copy-start.14
  261.6 1.6 copy-start.39
  279.0 39.7 %copy-start.6 = (bf16[2,128,3584]{2,1,0:T(8,128)(2,1)S(1)}, bf16[2,128,3584]{2,1,0:T(8,128)(2,1)}, u32[]{:S(2)}) copy-start(bf16[2,128,3584]{2,1,0:T(8,128)(2,1)} %param.17) | copy-start | bytes 5505028
  279.0 86.3 %copy-start.33 = (s32[1,3]{1,0:T(1,128)S(1)}, s32[1,3]{1,0:T(1,128)}, u32[]{:S(2)}) copy-start(s32[1,3]{1,0:T(1,128)} %param.16) | copy-start | bytes 40
  279.0 145.8 %copy-start.15 = (s32[1,3]{1,0:T(1,128)S(1)}, s32[1,3]{1,0:T(1,128)}, u32[]{:S(2)}) copy-start(s32[1,3]{1,0:T(1,128)} %param.15) | copy-start | bytes 40
  279.0 145.8 %copy-start.19 = (s32[3]{0:T(128)S(1)}, s32[3]{0:T(128)}, u32[]{:S(2)}) copy-start(s32[3]{0:T(128)} %copy-done.18) | copy-start | bytes 40
  279.0 145.8 %copy-start.20 = (s32[1024]{0:T(1024)S(1)}, s32[1024]{0:T(1024)}, u32[]{:S(2)}) copy-start(s32[1024]{0:T(1024)} %param.27) | copy-start | bytes 12292
  279.0 146.0 %copy-start.28 = (s32[3]{0:T(128)S(1)}, s32[3]{0:T(128)}, u32[]{:S(2)}) copy-start(s32[3]{0:T(128)} %copy-done.27) | copy-start | bytes 40
  279.0 146.0 %copy-start.30 = (s32[3]{0:T(128)S(1)}, s32[3]{0:T(128)}, u32[]{:S(2)}) copy-start(s32[3]{0:T(128)} %copy-done.29) | copy-start | bytes 40
  279.1 146.1 %copy-start.24 = (s32[3]{0:T(128)S(1)}, s32[3]{0:T(128)}, u32[]{:S(2)}) copy-start(s32[3]{0:T(128)} %copy-done.23) | copy-start | bytes 40
  279.1 146.2 %copy-start.26 = (s32[3]{0:T(128)S(1)}, s32[3]{0:T(128)}, u32[]{:S(2)}) copy-start(s32[3]{0:T(128)} %copy-done.25) | copy-start | bytes 40
  279.1 86.2 %all-gather.7.cloned.1.call-start = ((), (), s32[]{:S(2)}) async-start(), calls=%async_computation.5 | async-start | bytes 4587520 | tf_op jit(solution)/shard_map/all_gather | solution.py:118
  365.3 204.8 %collective-permute-start.2 = (bf16[512,3584]{1,0:T(8,128)(2,1)}, bf16[512,3584]{1,0:T(8,128)(2,1)}, u32[]{:S(2)}, u32[]{:S(2)}) collective-permute-start(bf16[512,3584]{1,0:T(8,128)(2,1)} %all-gather.7.cloned.1.call-done), channel_id=1, source_target_pairs={{124,0},{0,4},{4,8},{8,12},{12,16},{16,20},{20,24},{24,28},{28,32}... | collective-permute-start | bytes 11010056 | tf_op jit(solution)/shard_map/ppermute | solution.py:17
  365.3 45.9 %collective-permute-start.3 = (s32[3]{0:T(128)S(1)}, s32[3]{0:T(128)S(1)}, u32[]{:S(2)}, u32[]{:S(2)}) collective-permute-start(s32[3]{0:T(128)S(1)} %fusion.115), channel_id=1, source_target_pairs={{124,0},{0,4},{4,8},{8,12},{12,16},{16,20},{20,24},{24,28},{28,32}... | collective-permute-start | bytes 44 | tf_op jit(solution)/shard_map/ppermute | solution.py:17
Sparse Core Ops, SparseCore 0:
  9.7 46.3 all-gather.8
  98.7 42.7 reduce-scatter.2
  144.4 43.6 all-gather.4
  279.2 39.4 reduce-scatter.4
  321.6 43.6 all-gather.6
where the time goes:
time: 586 us; the launch traced here: 579 us
  waiting for transfers between devices  300 us (51%)
  blocking collectives  153 us (26%)
  matrix products  57.4 us (10%)
  other arithmetic  27.9 us (5%)
  local copies, waits for them, and re-layouts  23.6 us (4%)
  between operations  14.7 us (3%)
    psum x2, blocking collectives, broadcast(): return lax.psum(jnp.where(mine, value, jnp.zeros_like(value)), axis)  137 us
    all_gather x3, waiting for transfers between devices, assemble(): return lax.all_gather(rows, 'tensor', axis=0, tiled=True)  124 us
    ppermute x4, waiting for transfers between devices, from_behind(): return lax.ppermute(block, axis, route)  93 us
    reduce_scatter x2, waiting for transfers between devices, local(): lax.psum_scatter(jnp.dot(mixed, output_weight[0], preferred_element_type=...  82.4 us
    dot_general x2, matrix products, local(): jnp.dot(mixed, output_weight[0], preferred_element_type=jnp.float32)  16.6 us
    psum x1, blocking collectives, local(): total = lax.psum(parts.astype(jnp.bfloat16), 'tensor').astype(jnp.float32)  15.9 us
    dot_general x2, matrix products, one_block(): jnp.einsum('cgqk,kcd->qcgd', probs, value_rows, preferred_element_type=jn...  15.2 us
    unnamed x84, local copies, waits for them, and re-layouts  14.6 us
  transfers between devices with their start and end apart: 9, of which 8 were waited for; matrix products, arithmetic and copies ran while one was open for 2% of the time, Pallas kernels for 0%

commit v1 on v0

--- a/solution.py
+++ b/solution.py
@@ -9,6 +9,23 @@
 BLOCK = 128
 EPS = 1e-06
 THETA = 1000000.0
+
+
+def slots_draft(inp):
+    device_axis = "tensor"
+    axis_len = lax.psum(1, device_axis)
+    grid = [(num, (num + 1) % axis_len) for num in range(axis_len)]
+    rack = [(num, (num - 1) % axis_len) for num in range(axis_len)]
+    val2, local_next = ([inp], [inp])
+    for _ in range(axis_len // 2):
+        val2.append(lax.ppermute(val2[-1], device_axis, grid))
+    ii = 0
+    while ii < (axis_len - 1) // 2:
+        v1 = lax.ppermute(local_next[-1], device_axis, rack)
+        local_next.append(v1)
+        ii += 1
+    after = jnp.concatenate([*val2[::-1], *local_next[1:]], axis=0)
+    return jnp.roll(after, (lax.axis_index(device_axis) - axis_len // 2) * inp.shape[0], 0)
 
 
 def from_behind(block, axis, distance):
@@ -115,7 +132,7 @@
     prog_count = flight_tokens.shape[1]
 
     def assemble(rows):
-        return lax.all_gather(rows, "tensor", axis=0, tiled=True)
+        return slots_draft(rows)
 
     tokens = flight_tokens[0]
     lists = flight_lists[0]

time: 586 us -> 619 us (1.056)
  other arithmetic: 27.9 us -> 58.5 us
  waiting for transfers between devices: 300 us -> 290 us
  starting transfers between devices: 2 us -> 11.9 us
    all_gather x3 -> x0, waiting for transfers between devices: 124 us -> none  [assemble(): return lax.all_gather(rows, 'tensor', axis=0, tiled=True)]
    ppermute x0 -> x9, waiting for transfers between devices: none -> 119 us  [the longest x6 119 us: slots_draft(): val2.append(lax.ppermute(val2[-1], device_axis, grid))]
    concatenate x0 -> x3, other arithmetic: none -> 31.6 us  [slots_draft(): jnp.roll(after, (lax.axis_index(device_axis) - axis_len // 2) * inp.shape...]
    ppermute x0 -> x9, starting transfers between devices: none -> 10.1 us  [the longest x3 8.88 us: slots_draft(): v1 = lax.ppermute(local_next[-1], device_axis, rack)]
    unnamed x84 -> x90, local copies, waits for them, and re-layouts: 14.6 us -> 16.2 us
  transfers between devices with their start and end apart: 9 -> 15, of which waited for: 8 -> 11; matrix products, arithmetic and copies ran while one was open for 2% -> 3% of each run, Pallas kernels for 0% -> 0%
where the time goes in v1:
time: 619 us; the launch traced here: 612 us
  waiting for transfers between devices  290 us (47%)
  blocking collectives  152 us (25%)
  matrix products  59 us (10%)
  other arithmetic  58.5 us (9%)
  local copies, waits for them, and re-layouts  25.3 us (4%)
  between operations  14.9 us (2%)
  starting transfers between devices  11.9 us (2%)
    psum x2, blocking collectives, broadcast(): return lax.psum(jnp.where(mine, value, jnp.zeros_like(value)), axis)  137 us
    ppermute x6, waiting for transfers between devices, slots_draft(): val2.append(lax.ppermute(val2[-1], device_axis, grid))  119 us
    ppermute x4, waiting for transfers between devices, from_behind(): return lax.ppermute(block, axis, route)  90.3 us
    reduce_scatter x2, waiting for transfers between devices, local(): lax.psum_scatter(jnp.dot(mixed, output_weight[0], preferred_element_type=...  80.7 us
    concatenate x3, other arithmetic, slots_draft(): jnp.roll(after, (lax.axis_index(device_axis) - axis_len // 2) * inp.shape...  31.6 us
    dot_general x2, matrix products, local(): jnp.dot(mixed, output_weight[0], preferred_element_type=jnp.float32)  18.3 us
    dot_general x2, matrix products, one_block(): jnp.einsum('cgqk,kcd->qcgd', probs, value_rows, preferred_element_type=jn...  17 us
    unnamed x90, local copies, waits for them, and re-layouts  16.2 us
  transfers between devices with their start and end apart: 15, of which 11 were waited for; matrix products, arithmetic and copies ran while one was open for 3% of the time, Pallas kernels for 0%

profile of v1, /device:TPU:0, one launch (start us, length us, event | category | flops | bytes accessed | tf_op | source)
XLA Modules:
  0.0 611.7 jit_solution(16859063835080431067)
XLA Ops:
  7.2 2.9 collective-permute-start.2
  10.1 0.7 broadcast_select_fusion.1
  10.8 0.7 and_select_fusion.2
  11.7 0.7 fusion.130
  12.9 0.7 select_reduce_fusion.3
  14.2 1.3 reduce.5
  15.4 1.3 reduce.4
  17.1 0.6 collective-permute-done.7
  17.9 15.5 %collective-permute-done = bf16[128,3584]{1,0:T(8,128)(2,1)S(1)} collective-permute-done((bf16[128,3584]{1,0:T(8,128)(2,1)}, bf16[128,3584]{1,0:T(8,128)(2,1)S(1)}, u32[]{:S(2)}, u32[]{:S(2)}) %collective-permute-start) | collective-permute-done | bytes 917536 | tf_op jit(solution)/shard_map/ppermute | solution.py:21
  33.5 0.7 select_reduce_fusion.1
  34.2 3.3 multiply_cosine_fusion
  37.5 18.0 %collective-permute-done.1 = bf16[128,3584]{1,0:T(8,128)(2,1)S(1)} collective-permute-done((bf16[128,3584]{1,0:T(8,128)(2,1)S(1)}, bf16[128,3584]{1,0:T(8,128)(2,1)S(1)}, u32[]{:S(2)}, u32[]{:S(2)}) %collective-permute-start.1) | collective-permute-done | bytes 917536 | tf_op jit(solution)/shard_map/ppermute | solution.py:21
  55.5 3.1 maximum_maximum_fusion
  58.6 0.8 fusion
  59.4 1.5 fusion.61
  60.9 1.2 fusion.107
  62.2 5.4 fusion.46
  67.6 2.0 copy.34
  69.6 1.5 fusion.146
  71.1 1.7 copy.57
  72.8 3.1 copy.56
  75.8 2.1 subtract_convert_fusion.1
  77.9 2.9 fusion.22
  80.9 3.0 copy-done.2
  83.9 1.6 fusion.6
  85.5 8.5 %fusion.52 = bf16[128,7,512]{2,0,1:T(8,128)(2,1)} fusion(f32[7,512]{1,0:T(8,128)S(1)} %fusion.6, f32[7,512]{1,0:T(8,128)S(1)} %get-tuple-element.73, f32[512,512,7]{1,0,2:T(8,128)} %copy-done.2, pred[512,512]{0,1:T(8,128)(4,1)S(1)} %compare_and_fusion.1, bf16[1,3584,128]{2,1,0:T(8,128)(2,1)S(1)} %copy-done, f32[128]{0:T(128)S(1)} %bitcast.175, ...), kind=kOutput, calls=%fused_computation.79 | convolution fusion | flops 956628992 | bytes 13152772 | tf_op jit(solution)/shard_map/while/body/eval_jaxpr/cgqk,kcd->qcgd/dot_general | solution.py:88
  94.0 9.1 %fusion.16 = bf16[512,3584]{1,0:T(8,128)(2,1)} fusion(bf16[512,896]{0,1:T(8,128)(2,1)} %bitcast.178, bf16[1,896,3584]{2,1,0:T(8,128)(2,1)} %param.28), kind=kOutput, calls=%fused_computation.43 | convolution fusion | flops 3290169344 | bytes 11010048 | tf_op jit(solution)/shard_map/dot_general | solution.py:168
  103.3 42.5 %reduce-scatter.3.cloned.1.call-done = bf16[128,3584]{1,0:T(8,128)(2,1)} async-done(((bf16[512,3584]{1,0:T(8,128)(2,1)}), bf16[128,3584]{1,0:T(8,128)(2,1)}) %reduce-scatter.3.cloned.1.call-update) | async-done | bytes 917520 | tf_op jit(solution)/shard_map/reduce_scatter | solution.py:167
  145.8 2.1 bitcast_select_fusion.2
  147.8 0.7 collective-permute-start.3
  148.6 3.0 collective-permute-start.5
  151.6 20.1 %collective-permute-done.3 = bf16[128,3584]{1,0:T(8,128)(2,1)S(1)} collective-permute-done((bf16[128,3584]{1,0:T(8,128)(2,1)S(1)}, bf16[128,3584]{1,0:T(8,128)(2,1)S(1)}, u32[]{:S(2)}, u32[]{:S(2)}) %collective-permute-start.3) | collective-permute-done | bytes 917536 | tf_op jit(solution)/shard_map/ppermute | solution.py:21
  171.7 22.5 %collective-permute-done.4 = bf16[128,3584]{1,0:T(8,128)(2,1)S(1)} collective-permute-done((bf16[128,3584]{1,0:T(8,128)(2,1)S(1)}, bf16[128,3584]{1,0:T(8,128)(2,1)S(1)}, u32[]{:S(2)}, u32[]{:S(2)}) %collective-permute-start.4) | collective-permute-done | bytes 917536 | tf_op jit(solution)/shard_map/ppermute | solution.py:21
  194.1 15.4 %fusion.36 = bf16[512,3584]{1,0:T(8,128)(2,1)S(1)} fusion(s32[]{:T(128)S(6)} %select_n.164, bf16[128,3584]{1,0:T(8,128)(2,1)S(1)} %collective-permute-done.4, bf16[128,3584]{1,0:T(8,128)(2,1)S(1)} %collective-permute-done.3, bf16[128,3584]{1,0:T(8,128)(2,1)S(1)} %bitcast_select_fusion.2, bf16[128,3584]{1,0:T(8,128)(2,1)S(1)} %collective-permute-done.5), kind=kLoop, calls=%fused_computation.61 | loop fusion | flops 29360128 | bytes 7340036 | tf_op jit(solution)/shard_map/jit(_roll_dynamic)/concatenate | solution.py:28
  209.9 45.3 %collective-permute-done.6 = bf16[512,3584]{1,0:T(8,128)(2,1)S(1)} collective-permute-done((bf16[512,3584]{1,0:T(8,128)(2,1)S(1)}, bf16[512,3584]{1,0:T(8,128)(2,1)S(1)}, u32[]{:S(2)}, u32[]{:S(2)}) %collective-permute-start.6) | collective-permute-done | bytes 3670048 | tf_op jit(solution)/shard_map/ppermute | solution.py:34
  255.3 0.8 fusion.3
  256.1 1.5 fusion.60
  257.6 1.2 fusion.109
  258.8 5.4 fusion.49
  264.2 2.0 copy.40
  266.2 1.5 fusion.145
  267.6 1.7 copy.59
  269.4 3.1 copy.58
  272.4 2.0 subtract_convert_fusion
  274.4 2.9 fusion.23
  277.4 3.0 copy-done.1
  280.4 1.6 fusion.7
  282.0 8.5 %fusion.55 = bf16[128,7,512]{2,0,1:T(8,128)(2,1)} fusion(f32[7,512]{1,0:T(8,128)S(1)} %fusion.7, f32[7,512]{1,0:T(8,128)S(1)} %get-tuple-element.75, f32[512,512,7]{1,0,2:T(8,128)} %copy-done.1, pred[512,512]{0,1:T(8,128)(4,1)S(1)} %compare_and_fusion, bf16[1,3584,128]{2,1,0:T(8,128)(2,1)S(1)} %copy-done, f32[128]{0:T(128)S(1)} %bitcast.176, ...), kind=kOutput, calls=%fused_computation.80 | convolution fusion | flops 956628992 | bytes 13152768 | tf_op jit(solution)/shard_map/while/body/eval_jaxpr/cgqk,kcd->qcgd/dot_general | solution.py:88
  290.5 9.1 %fusion.19 = bf16[512,3584]{1,0:T(8,128)(2,1)} fusion(bf16[512,896]{0,1:T(8,128)(2,1)} %bitcast.177, bf16[1,896,3584]{2,1,0:T(8,128)(2,1)} %param.28), kind=kOutput, calls=%fused_computation.44 | convolution fusion | flops 3290169344 | bytes 11010048 | tf_op jit(solution)/shard_map/dot_general | solution.py:168
  299.7 38.2 %reduce-scatter.5.cloned.1.call-done = bf16[128,3584]{1,0:T(8,128)(2,1)} async-done(((bf16[512,3584]{1,0:T(8,128)(2,1)}), bf16[128,3584]{1,0:T(8,128)(2,1)}) %reduce-scatter.5.cloned.1.call-update) | async-done | bytes 917520 | tf_op jit(solution)/shard_map/reduce_scatter | solution.py:167
  337.9 1.8 bitcast_select_fusion.3
  340.3 3.0 collective-permute-start.10
  343.3 20.1 %collective-permute-done.8 = bf16[128,3584]{1,0:T(8,128)(2,1)S(1)} collective-permute-done((bf16[128,3584]{1,0:T(8,128)(2,1)S(1)}, bf16[128,3584]{1,0:T(8,128)(2,1)S(1)}, u32[]{:S(2)}, u32[]{:S(2)}) %collective-permute-start.8) | collective-permute-done | bytes 917536 | tf_op jit(solution)/shard_map/ppermute | solution.py:21
  363.5 22.5 %collective-permute-done.9 = bf16[128,3584]{1,0:T(8,128)(2,1)S(1)} collective-permute-done((bf16[128,3584]{1,0:T(8,128)(2,1)S(1)}, bf16[128,3584]{1,0:T(8,128)(2,1)S(1)}, u32[]{:S(2)}, u32[]{:S(2)}) %collective-permute-start.9) | collective-permute-done | bytes 917536 | tf_op jit(solution)/shard_map/ppermute | solution.py:21
  386.0 13.2 %fusion.29 = bf16[512,3584]{1,0:T(8,128)(2,1)} fusion(s32[]{:T(128)S(6)} %select_n.164, bf16[128,3584]{1,0:T(8,128)(2,1)S(1)} %collective-permute-done.9, bf16[128,3584]{1,0:T(8,128)(2,1)S(1)} %collective-permute-done.8, bf16[128,3584]{1,0:T(8,128)(2,1)S(1)} %bitcast_select_fusion.3, bf16[128,3584]{1,0:T(8,128)(2,1)S(1)} %collective-permute-done.10), kind=kLoop, calls=%fused_computation.54 | loop fusion | flops 29360128 | bytes 7340036 | tf_op jit(solution)/shard_map/jit(_roll_dynamic)/concatenate | solution.py:28
  399.1 1.6 collective-permute-start.12
  400.7 44.3 %collective-permute-done.12 = s32[3]{0:T(128)S(1)} collective-permute-done((s32[3]{0:T(128)S(1)}, s32[3]{0:T(128)S(1)}, u32[]{:S(2)}, u32[]{:S(2)}) %collective-permute-start.12) | collective-permute-done | bytes 44 | tf_op jit(solution)/shard_map/ppermute | solution.py:34
  445.2 13.5 %psum.21 = s32[6]{0:T(128)S(1)} all-reduce(s32[6]{0:T(128)S(1)} %eq.175), channel_id=1, replica_groups=mesh['section'=32,'tensor'=4] {'section'}, use_global_device_ids=true, to_apply=%region_16.18 | all-reduce | flops 6 | bytes 48 | tf_op jit(solution)/shard_map/psum | solution.py:39
  459.2 1.7 fusion.24
  460.9 1.6 fusion.25
  462.5 14.9 %psum.22 = bf16[2,3,3584]{2,1,0:T(4,128)(2,1)S(1)} all-reduce(bf16[2,3,3584]{2,1,0:T(4,128)(2,1)S(1)} %pad_maximum_fusion), channel_id=1, replica_groups=mesh['section'=32,'tensor'=4] {'tensor'}, use_global_device_ids=true, to_apply=%region_24.26 | all-reduce | flops 21504 | bytes 86016 | tf_op jit(solution)/shard_map/psum | solution.py:194
  477.8 123.9 %psum.23 = bf16[6,3584]{1,0:T(8,128)(2,1)S(1)} all-reduce(bf16[6,3584]{1,0:T(8,128)(2,1)S(1)} %reshape.609), channel_id=1, replica_groups=mesh['section'=32,'tensor'=4] {'section'}, use_global_device_ids=true, to_apply=%region_26.28 | all-reduce | flops 21504 | bytes 86016 | tf_op jit(solution)/shard_map/psum | solution.py:39
  601.6 0.8 fusion.113
  602.5 2.2 dynamic-slice_bitcast_fusion
  (135 shorter events, 4.0 us)
Async XLA Ops:
  7.2 78.3 %copy-start = (bf16[1,3584,128]{2,1,0:T(8,128)(2,1)S(1)}, bf16[1,3584,128]{2,1,0:T(8,128)(2,1)}, u32[]{:S(2)}) copy-start(bf16[1,3584,128]{2,1,0:T(8,128)(2,1)} %param.26) | copy-start | bytes 2752516
  7.2 138.6 %reduce-scatter.3.cloned.1.call-start = ((), (), s32[]{:S(2)}) async-start(), calls=%async_computation.2 | async-start | bytes 4587520 | tf_op jit(solution)/shard_map/reduce_scatter | solution.py:167
  7.2 30.2 %collective-permute-start.2 = (bf16[128,3584]{1,0:T(8,128)(2,1)}, bf16[128,3584]{1,0:T(8,128)(2,1)S(1)}, u32[]{:S(2)}, u32[]{:S(2)}) collective-permute-start(bf16[128,3584]{1,0:T(8,128)(2,1)} %bitcast.162), channel_id=1, source_target_pairs={{0,3},{1,0},{2,1},{3,2},{4,7},{5,4},{6,5},{7,6},{8,11},{9,8},{10,9... | collective-permute-start | bytes 2752520 | tf_op jit(solution)/shard_map/ppermute | solution.py:24
  10.1 23.2 %collective-permute-start = (bf16[128,3584]{1,0:T(8,128)(2,1)}, bf16[128,3584]{1,0:T(8,128)(2,1)S(1)}, u32[]{:S(2)}, u32[]{:S(2)}) collective-permute-start(bf16[128,3584]{1,0:T(8,128)(2,1)} %bitcast.163), channel_id=1, source_target_pairs={{0,1},{1,2},{2,3},{3,0},{4,5},{5,6},{6,7},{7,4},{8,9},{9,10},{10,1... | collective-permute-start | bytes 2752520 | tf_op jit(solution)/shard_map/ppermute | solution.py:21
  10.8 6.9 %collective-permute-start.7 = (s32[3]{0:T(128)S(1)}, s32[3]{0:T(128)S(1)}, u32[]{:S(2)}, u32[]{:S(2)}) collective-permute-start(s32[3]{0:T(128)S(1)} %broadcast_select_fusion.1), channel_id=1, source_target_pairs={{124,0},{0,4},{4,8},{8,12},{12,16},{16,20},{20,24},{24,28},{28,32}... | collective-permute-start | bytes 44 | tf_op jit(solution)/shard_map/ppermute | solution.py:34
  12.3 4.5 copy-start.22
  12.4 0.5 copy-start.26
  17.7 16.5 %copy-start.17 = (s32[3]{0:T(128)}, s32[3]{0:T(128)S(1)}, u32[]{:S(2)}) copy-start(s32[3]{0:T(128)S(1)} %collective-permute-done.7) | copy-start | bytes 40
  17.9 15.5 %copy-start.28 = (s32[3]{0:T(128)}, s32[3]{0:T(128)S(1)}, u32[]{:S(2)}) copy-start(s32[3]{0:T(128)S(1)} %multiply_bitcast_fusion) | copy-start | bytes 40
  33.4 22.1 %collective-permute-start.1 = (bf16[128,3584]{1,0:T(8,128)(2,1)S(1)}, bf16[128,3584]{1,0:T(8,128)(2,1)S(1)}, u32[]{:S(2)}, u32[]{:S(2)}) collective-permute-start(bf16[128,3584]{1,0:T(8,128)(2,1)S(1)} %collective-permute-done), channel_id=1, source_target_pairs={{0,1},{1,2},{2,3},{3,0},{4,5},{5,6},{6,7},{7,4},{8,9},{9,10},{10,1... | collective-permute-start | bytes 2752520 | tf_op jit(solution)/shard_map/ppermute | solution.py:21
  33.5 0.7 copy-start.24
  37.5 21.9 %copy-start.9 = (f32[3584]{0:T(1024)S(1)}, f32[3584]{0:T(1024)}, u32[]{:S(2)}) copy-start(f32[3584]{0:T(1024)} %reduce.4) | copy-start | bytes 43012
  37.5 22.0 %copy-start.33 = (bf16[1,3584,128]{2,1,0:T(8,128)(2,1)S(1)}, bf16[1,3584,128]{2,1,0:T(8,128)(2,1)}, u32[]{:S(2)}) copy-start(bf16[1,3584,128]{2,1,0:T(8,128)(2,1)} %param.24) | copy-start | bytes 2752516
  37.5 22.0 %copy-start.35 = (f32[1,128]{1,0:T(1,128)S(1)}, f32[1,128]{1,0:T(1,128)}, u32[]{:S(2)}) copy-start(f32[1,128]{1,0:T(1,128)} %param.25) | copy-start | bytes 1540
  55.5 6.7 %slice-start = ((s8[6422528]{0:T(1024)(128)(4,1)}), s8[4194304]{0:T(1024)(128)(4,1)S(1)}, s32[]{:S(2)}) async-start(s8[6422528]{0:T(1024)(128)(4,1)} %bitcast.169), calls=%async_computation.4 | async-start | bytes 8388608
  58.5 3.6 copy-start.3
  58.6 2.4 copy-start.15
  58.6 3.6 copy-start.20
  58.6 3.6 slice-start.1
  59.4 2.8 copy-start.30
  77.9 7.6 %copy-start.10 = (f32[3584]{0:T(1024)S(1)}, f32[3584]{0:T(1024)}, u32[]{:S(2)}) copy-start(f32[3584]{0:T(1024)} %reduce.4) | copy-start | bytes 43012
  77.9 7.6 %copy-start.31 = (f32[512]{0:T(512)S(1)}, f32[512]{0:T(512)}, u32[]{:S(2)}) copy-start(f32[512]{0:T(512)} %copy-done.30) | copy-start | bytes 6148
  77.9 7.6 %copy-start.37 = (f32[1,128]{1,0:T(1,128)S(1)}, f32[1,128]{1,0:T(1,128)}, u32[]{:S(2)}) copy-start(f32[1,128]{1,0:T(1,128)} %param.27) | copy-start | bytes 1540
  80.9 3.0 copy-start.2
  94.0 51.7 %copy-start.5 = (bf16[2,128,3584]{2,1,0:T(8,128)(2,1)S(1)}, bf16[2,128,3584]{2,1,0:T(8,128)(2,1)}, u32[]{:S(2)}) copy-start(bf16[2,128,3584]{2,1,0:T(8,128)(2,1)} %param.19) | copy-start | bytes 5505028
  103.2 106.5 %copy-start.14 = (s32[512]{0:T(512)S(1)}, s32[512]{0:T(512)}, u32[]{:S(2)}) copy-start(s32[512]{0:T(512)} %get-tuple-element.31) | copy-start | bytes 6148
  103.2 234.7 %reduce-scatter.5.cloned.1.call-start = ((), (), s32[]{:S(2)}) async-start(), calls=%async_computation.3 | async-start | bytes 4587520 | tf_op jit(solution)/shard_map/reduce_scatter | solution.py:167
  145.8 110.3 %copy-start.11 = (f32[3584]{0:T(1024)S(1)}, f32[3584]{0:T(1024)}, u32[]{:S(2)}) copy-start(f32[3584]{0:T(1024)} %reduce.4) | copy-start | bytes 43012
  145.8 110.3 %copy-start.34 = (bf16[1,3584,128]{2,1,0:T(8,128)(2,1)S(1)}, bf16[1,3584,128]{2,1,0:T(8,128)(2,1)}, u32[]{:S(2)}) copy-start(bf16[1,3584,128]{2,1,0:T(8,128)(2,1)} %param.24) | copy-start | bytes 2752516
  145.8 110.3 %copy-start.36 = (f32[1,128]{1,0:T(1,128)S(1)}, f32[1,128]{1,0:T(1,128)}, u32[]{:S(2)}) copy-start(f32[1,128]{1,0:T(1,128)} %param.25) | copy-start | bytes 1540
  147.8 23.8 %collective-permute-start.3 = (bf16[128,3584]{1,0:T(8,128)(2,1)S(1)}, bf16[128,3584]{1,0:T(8,128)(2,1)S(1)}, u32[]{:S(2)}, u32[]{:S(2)}) collective-permute-start(bf16[128,3584]{1,0:T(8,128)(2,1)S(1)} %bitcast_select_fusion.2), channel_id=1, source_target_pairs={{0,1},{1,2},{2,3},{3,0},{4,5},{5,6},{6,7},{7,4},{8,9},{9,10},{10,1... | collective-permute-start | bytes 2752520 | tf_op jit(solution)/shard_map/ppermute | solution.py:21
  148.6 23.1 %collective-permute-start.5 = (bf16[128,3584]{1,0:T(8,128)(2,1)S(1)}, bf16[128,3584]{1,0:T(8,128)(2,1)S(1)}, u32[]{:S(2)}, u32[]{:S(2)}) collective-permute-start(bf16[128,3584]{1,0:T(8,128)(2,1)S(1)} %bitcast_select_fusion.2), channel_id=1, source_target_pairs={{0,3},{1,0},{2,1},{3,2},{4,7},{5,4},{6,5},{7,6},{8,11},{9,8},{10,9... | collective-permute-start | bytes 2752520 | tf_op jit(solution)/shard_map/ppermute | solution.py:24
  171.7 22.5 %collective-permute-start.4 = (bf16[128,3584]{1,0:T(8,128)(2,1)S(1)}, bf16[128,3584]{1,0:T(8,128)(2,1)S(1)}, u32[]{:S(2)}, u32[]{:S(2)}) collective-permute-start(bf16[128,3584]{1,0:T(8,128)(2,1)S(1)} %collective-permute-done.3), channel_id=1, source_target_pairs={{0,1},{1,2},{2,3},{3,0},{4,5},{5,6},{6,7},{7,4},{8,9},{9,10},{10,1... | collective-permute-start | bytes 2752520 | tf_op jit(solution)/shard_map/ppermute | solution.py:21
  209.5 48.1 %copy-start.16 = (f32[64]{0:T(128)S(1)}, f32[64]{0:T(128)}, u32[]{:S(2)}) copy-start(f32[64]{0:T(128)} %multiply_power_fusion) | copy-start | bytes 772
  209.5 49.3 %copy-start.21 = (f32[896]{0:T(1024)S(1)}, f32[896]{0:T(1024)}, u32[]{:S(2)}) copy-start(f32[896]{0:T(1024)} %reduce.5) | copy-start | bytes 10756
  209.6 49.3 %slice-start.2 = ((s8[6422528]{0:T(1024)(128)(4,1)}), s8[4194304]{0:T(1024)(128)(4,1)S(1)}, s32[]{:S(2)}) async-start(s8[6422528]{0:T(1024)(128)(4,1)} %bitcast.171), calls=%async_computation.6 | async-start | bytes 8388608
  209.6 45.7 %collective-permute-start.6 = (bf16[512,3584]{1,0:T(8,128)(2,1)S(1)}, bf16[512,3584]{1,0:T(8,128)(2,1)S(1)}, u32[]{:S(2)}, u32[]{:S(2)}) collective-permute-start(bf16[512,3584]{1,0:T(8,128)(2,1)S(1)} %fusion.36), channel_id=1, source_target_pairs={{124,0},{0,4},{4,8},{8,12},{12,16},{16,20},{20,24},{24,28},{28,32}... | collective-permute-start | bytes 11010056 | tf_op jit(solution)/shard_map/ppermute | solution.py:34
  255.3 3.5 copy-start.4
  256.1 2.7 slice-start.3
  274.4 7.6 %copy-start.12 = (f32[3584]{0:T(1024)S(1)}, f32[3584]{0:T(1024)}, u32[]{:S(2)}) copy-start(f32[3584]{0:T(1024)} %reduce.4) | copy-start | bytes 43012
  274.4 7.6 %copy-start.38 = (f32[1,128]{1,0:T(1,128)S(1)}, f32[1,128]{1,0:T(1,128)}, u32[]{:S(2)}) copy-start(f32[1,128]{1,0:T(1,128)} %param.27) | copy-start | bytes 1540
  277.4 3.0 copy-start.1
  290.5 47.5 %copy-start.6 = (bf16[2,128,3584]{2,1,0:T(8,128)(2,1)S(1)}, bf16[2,128,3584]{2,1,0:T(8,128)(2,1)}, u32[]{:S(2)}) copy-start(bf16[2,128,3584]{2,1,0:T(8,128)(2,1)} %param.19) | copy-start | bytes 5505028
  299.6 99.5 %copy-start.32 = (s32[1,3]{1,0:T(1,128)S(1)}, s32[1,3]{1,0:T(1,128)}, u32[]{:S(2)}) copy-start(s32[1,3]{1,0:T(1,128)} %param.18) | copy-start | bytes 40
  299.6 159.0 %copy-start.13 = (s32[1,3]{1,0:T(1,128)S(1)}, s32[1,3]{1,0:T(1,128)}, u32[]{:S(2)}) copy-start(s32[1,3]{1,0:T(1,128)} %param.17) | copy-start | bytes 40
  299.6 159.0 %copy-start.18 = (s32[3]{0:T(128)S(1)}, s32[3]{0:T(128)}, u32[]{:S(2)}) copy-start(s32[3]{0:T(128)} %copy-done.17) | copy-start | bytes 40
  299.6 159.0 %copy-start.19 = (s32[1024]{0:T(1024)S(1)}, s32[1024]{0:T(1024)}, u32[]{:S(2)}) copy-start(s32[1024]{0:T(1024)} %param.29) | copy-start | bytes 12292
  299.6 159.2 %copy-start.27 = (s32[3]{0:T(128)S(1)}, s32[3]{0:T(128)}, u32[]{:S(2)}) copy-start(s32[3]{0:T(128)} %copy-done.26) | copy-start | bytes 40
  299.7 159.2 %copy-start.29 = (s32[3]{0:T(128)S(1)}, s32[3]{0:T(128)}, u32[]{:S(2)}) copy-start(s32[3]{0:T(128)} %copy-done.28) | copy-start | bytes 40
  299.7 159.3 %copy-start.23 = (s32[3]{0:T(128)S(1)}, s32[3]{0:T(128)}, u32[]{:S(2)}) copy-start(s32[3]{0:T(128)} %copy-done.22) | copy-start | bytes 40
  299.7 159.4 %copy-start.25 = (s32[3]{0:T(128)S(1)}, s32[3]{0:T(128)}, u32[]{:S(2)}) copy-start(s32[3]{0:T(128)} %copy-done.24) | copy-start | bytes 40
  339.8 119.4 %copy-start.7 = (bf16[128,3584]{1,0:T(8,128)(2,1)S(1)}, bf16[128,3584]{1,0:T(8,128)(2,1)}, u32[]{:S(2)}) copy-start(bf16[128,3584]{1,0:T(8,128)(2,1)} %reduce-scatter.3.cloned.1.call-done) | copy-start | bytes 2752516
  339.8 121.1 %copy-start.8 = (bf16[128,3584]{1,0:T(8,128)(2,1)S(1)}, bf16[128,3584]{1,0:T(8,128)(2,1)}, u32[]{:S(2)}) copy-start(bf16[128,3584]{1,0:T(8,128)(2,1)} %reduce-scatter.5.cloned.1.call-done) | copy-start | bytes 2752516
  339.8 23.6 %collective-permute-start.8 = (bf16[128,3584]{1,0:T(8,128)(2,1)S(1)}, bf16[128,3584]{1,0:T(8,128)(2,1)S(1)}, u32[]{:S(2)}, u32[]{:S(2)}) collective-permute-start(bf16[128,3584]{1,0:T(8,128)(2,1)S(1)} %bitcast_select_fusion.3), channel_id=1, source_target_pairs={{0,1},{1,2},{2,3},{3,0},{4,5},{5,6},{6,7},{7,4},{8,9},{9,10},{10,1... | collective-permute-start | bytes 2752520 | tf_op jit(solution)/shard_map/ppermute | solution.py:21
  340.3 23.1 %collective-permute-start.10 = (bf16[128,3584]{1,0:T(8,128)(2,1)S(1)}, bf16[128,3584]{1,0:T(8,128)(2,1)S(1)}, u32[]{:S(2)}, u32[]{:S(2)}) collective-permute-start(bf16[128,3584]{1,0:T(8,128)(2,1)S(1)} %bitcast_select_fusion.3), channel_id=1, source_target_pairs={{0,3},{1,0},{2,1},{3,2},{4,7},{5,4},{6,5},{7,6},{8,11},{9,8},{10,9... | collective-permute-start | bytes 2752520 | tf_op jit(solution)/shard_map/ppermute | solution.py:24
  363.5 22.5 %collective-permute-start.9 = (bf16[128,3584]{1,0:T(8,128)(2,1)S(1)}, bf16[128,3584]{1,0:T(8,128)(2,1)S(1)}, u32[]{:S(2)}, u32[]{:S(2)}) collective-permute-start(bf16[128,3584]{1,0:T(8,128)(2,1)S(1)} %collective-permute-done.8), channel_id=1, source_target_pairs={{0,1},{1,2},{2,3},{3,0},{4,5},{5,6},{6,7},{7,4},{8,9},{9,10},{10,1... | collective-permute-start | bytes 2752520 | tf_op jit(solution)/shard_map/ppermute | solution.py:21
  399.1 203.3 %collective-permute-start.11 = (bf16[512,3584]{1,0:T(8,128)(2,1)}, bf16[512,3584]{1,0:T(8,128)(2,1)}, u32[]{:S(2)}, u32[]{:S(2)}) collective-permute-start(bf16[512,3584]{1,0:T(8,128)(2,1)} %fusion.29), channel_id=1, source_target_pairs={{124,0},{0,4},{4,8},{8,12},{12,16},{16,20},{20,24},{24,28},{28,32}... | collective-permute-start | bytes 11010056 | tf_op jit(solution)/shard_map/ppermute | solution.py:34
  399.1 45.9 %collective-permute-start.12 = (s32[3]{0:T(128)S(1)}, s32[3]{0:T(128)S(1)}, u32[]{:S(2)}, u32[]{:S(2)}) collective-permute-start(s32[3]{0:T(128)S(1)} %fusion.129), channel_id=1, source_target_pairs={{124,0},{0,4},{4,8},{8,12},{12,16},{16,20},{20,24},{24,28},{28,32}... | collective-permute-start | bytes 44 | tf_op jit(solution)/shard_map/ppermute | solution.py:34
Sparse Core Ops, SparseCore 0:
  103.3 42.4 reduce-scatter.2
  299.8 38.0 reduce-scatter.4
